TPU v7x, 256 devices: a whole 4x4x8 slice. The times are simulated.
256 devices in a mesh: row: 16 (over z, core), col: 16 (over x, y).
Axes of the slice: x: 4, y: 4, z: 8, core: 2. Of those that a mesh axis runs over, the one named last changes fastest.
Arguments:
- prior_factor: float32 [1024, 196608], P('row', 'col'), may hold values from -0.013671875 to 0.013671875
- prior_solution: float32 [64, 196608], P(None, 'col'), may hold values from -6 to 6
- panel_lower: float32 [1024, 1024], P('row'), may hold values from -1 to 1, as said below
- tile_inverse: float32 [1024, 64], P('row'), may hold values from -1 to 2, as said below
- panel_target: float32 [64, 1024], P(None, 'row'), may hold values from -6 to 6
- next_prior: float32 [1024, 196608], P('row', 'col'), may hold values from -0.013671875 to 0.013671875
- next_under: float32 [1024, 1024], P('row', 'col'), may hold values from -0.1875 to 0.1875
- next_target: float32 [64, 1024], P(None, 'row'), may hold values from -6 to 6
Outputs:
- panel_solution: float32 [64, 1024], P(None, 'row')
- next_remainder: float32 [64, 1024], P(None, 'row')
Inputs may be any that keep to these rules, and one draw needn't show every extreme that they name: `panel_lower`: zero in every column of the tile that holds the row and in all later columns; the other entries are independent. `tile_inverse`: each tile is lower triangular with diagonal entries between 0.6 and 1.6.
All inputs are finite; a program needn't handle non-finite values.
Results may differ from a plain program's by a relative error of at most 0.00011.
Values sent between devices are 32-bit elements; how exact they have to be, the bound alone decides.
A program may use at most 64 MiB of HBM per device.

v0:
```python
import jax
import jax.numpy as jnp
from jax import lax
from jax.sharding import PartitionSpec as P


def contract(left, right):
    return lax.dot_general(
        left,
        right,
        (((1,), (1,)), ((), ())),
        precision=lax.Precision.HIGHEST,
        preferred_element_type=jnp.float32,
    )


def solve_rows(target, lower_own, inverse_rows):
    tile = inverse_rows.shape[1]
    pieces = []
    for index in range(target.shape[1] // tile):
        first = index * tile
        current = target[:, first : first + tile]
        if index > 0:
            current = current - contract(
                jnp.concatenate(pieces, axis=1), lower_own[first : first + tile, :first]
            )
        pieces.append(contract(current, inverse_rows[first : first + tile, :]))
    return jnp.concatenate(pieces, axis=1)


def local(
    prior_factor,
    prior_solution,
    panel_lower,
    tile_inverse,
    panel_target,
    next_prior,
    next_under,
    next_target,
):
    rows_here = panel_target.shape[1]
    my_row = lax.axis_index("row")
    earlier = contract(prior_solution, prior_factor)
    next_part = contract(prior_solution, next_prior)
    panel_sum, next_sum = lax.psum((earlier, next_part), "col")
    remaining = panel_target - panel_sum
    whole_lower, whole_inverse, whole_target = (
        lax.all_gather(panel_lower, "row", axis=0, tiled=True),
        lax.all_gather(tile_inverse, "row", axis=0, tiled=True),
        lax.all_gather(remaining, "row", axis=1, tiled=True),
    )
    solved = solve_rows(whole_target, whole_lower, whole_inverse)
    own_solution = lax.dynamic_slice_in_dim(solved, my_row * rows_here, rows_here, 1)
    width = next_under.shape[1]
    solution_cols = lax.dynamic_slice_in_dim(solved, lax.axis_index("col") * width, width, 1)
    panel_part = contract(solution_cols, next_under)
    later = lax.psum(panel_part, "col")
    remainder = next_target - next_sum - later
    return (own_solution, remainder)


def solution(mesh):
    return jax.shard_map(
        local,
        mesh=mesh,
        in_specs=(
            P("row", "col"),
            P(None, "col"),
            P("row", None),
            P("row", None),
            P(None, "row"),
            P("row", "col"),
            P("row", "col"),
            P(None, "row"),
        ),
        out_specs=(P(None, "row"), P(None, "row")),
        check_vma=False,
    )
```

profile of v0, /device:TPU:32, one launch (start us, length us, event | category | flops | bytes accessed | tf_op | source)
XLA Modules:
  0.0 258.4 jit_solution(4807250656279358908)
XLA Ops:
  7.2 0.0 copy-start
  7.2 0.0 copy-start.3
  7.2 0.0 copy-start.4
  7.2 0.0 all-gather.2.cloned.1.call-start
  7.2 0.7 all-gather.2.cloned.1.call-update
  7.9 1.1 copy-done
  9.1 4.5 %fusion.69 = f32[64,64]{1,0:T(8,128)S(1)} fusion(f32[64,12288]{1,0:T(8,128)S(1)} %copy-done, f32[64,12288]{1,0:T(8,128)} %param.8), kind=kOutput, calls=%fused_computation.86 | convolution fusion | flops 603979776 | bytes 6307840 | tf_op jit(solution)/shard_map/dot_general | solution.py:8
  13.6 74.6 %psum.21 = f32[64,64]{1,0:T(8,128)S(1)} all-reduce(f32[64,64]{1,0:T(8,128)S(1)} %fusion.69), channel_id=1, replica_groups=mesh['row'=16,'col'=16] {'col'}, use_global_device_ids=true, to_apply=%region_0.0 | all-reduce | flops 4096 | bytes 32768 | tf_op jit(solution)/shard_map/psum | solution.py:45
  88.2 0.0 copy-done.3
  88.2 0.1 copy.10
  88.3 19.3 %all_gather.9 = f32[64,1024]{0,1:T(8,128)S(1)} all-gather(f32[64,64]{0,1:T(8,128)S(1)} %copy.10), channel_id=1, replica_groups=mesh['row'=16,'col'=16] {'row'}, dimensions={1}, use_global_device_ids=true | all-gather | bytes 278528 | tf_op jit(solution)/shard_map/all_gather | solution.py:50
  107.6 0.0 copy-done.4
  107.6 0.0 copy-start.2
  107.6 17.9 %all_gather.10 = f32[1024,64]{1,0:T(8,128)S(1)} all-gather(f32[64,64]{1,0:T(8,128)S(1)} %copy-done.4), channel_id=1, replica_groups=mesh['row'=16,'col'=16] {'row'}, dimensions={0}, use_global_device_ids=true | all-gather | bytes 278528 | tf_op jit(solution)/shard_map/all_gather | solution.py:49
  125.5 0.0 copy-done.2
  125.5 0.8 copy-done.1
  126.3 0.2 fusion.57
  126.6 5.1 %fusion.70 = f32[64,64]{1,0:T(8,128)} fusion(f32[64,12288]{1,0:T(8,128)S(1)} %copy-done, f32[64,12288]{1,0:T(8,128)} %param.13), kind=kOutput, calls=%fused_computation.87 | convolution fusion | flops 603979776 | bytes 6307840 | tf_op jit(solution)/shard_map/dot_general | solution.py:8
  131.7 1.0 convolution_subtract_fusion.9
  132.7 1.0 fusion.54
  133.7 1.0 convolution_subtract_fusion.8
  134.7 1.0 fusion.51
  135.7 1.1 convolution_subtract_fusion.7
  136.8 1.0 fusion.49
  137.8 1.1 convolution_subtract_fusion.6
  139.0 1.0 fusion.47
  140.0 0.1 concatenate.48
  140.1 1.2 convolution_subtract_fusion.5
  141.2 1.0 fusion.45
  142.2 0.1 concatenate.49
  142.3 1.2 convolution_subtract_fusion.4
  143.5 1.0 fusion.43
  144.5 0.1 concatenate.50
  144.6 1.2 convolution_subtract_fusion.3
  145.8 1.0 fusion.41
  146.8 0.1 concatenate.51
  146.9 1.2 convolution_subtract_fusion.2
  148.1 1.0 fusion.39
  149.1 0.8 concatenate.52
  149.8 1.3 convolution_subtract_fusion.1
  151.1 1.0 fusion.37
  152.1 0.8 concatenate.53
  152.9 1.3 convolution_subtract_fusion
  154.2 1.0 fusion.35
  155.2 0.8 concatenate.54
  156.0 1.3 convolution_subtract_fusion.14
  157.3 1.0 fusion.33
  158.3 0.8 concatenate.55
  159.1 1.3 convolution_subtract_fusion.13
  160.5 1.6 fusion.31
  162.1 1.6 concatenate.56
  163.6 1.4 convolution_subtract_fusion.12
  165.1 1.6 fusion.29
  166.7 1.6 concatenate.57
  168.3 1.4 convolution_subtract_fusion.11
  169.7 1.6 fusion.27
  171.3 1.6 concatenate.58
  172.9 1.4 convolution_subtract_fusion.10
  174.3 1.6 fusion.25
  175.9 1.6 concatenate.59
  177.5 1.4 constant_dynamic-slice_fusion
  179.0 1.0 fusion.63
  180.0 70.1 %all-reduce = (f32[64,64]{1,0:T(8,128)S(1)}, f32[64,64]{1,0:T(8,128)S(1)}) all-reduce(f32[64,64]{1,0:T(8,128)S(1)} %fusion.63, f32[64,64]{1,0:T(8,128)} %fusion.70), channel_id=1, replica_groups=mesh['row'=16,'col'=16] {'col'}, use_global_device_ids=true, to_apply=%region_2.0 | all-reduce | flops 8192 | bytes 65536 | tf_op jit(solution)/shard_map/psum | solution.py:57
  250.1 1.4 subtract_subtract_fusion
  (3 shorter events, 0.0 us)
Async XLA Ops:
  7.2 1.9 copy-start
  7.2 81.0 %copy-start.3 = (f32[64,64]{1,0:T(8,128)S(1)}, f32[64,64]{1,0:T(8,128)}, u32[]{:S(2)}) copy-start(f32[64,64]{1,0:T(8,128)} %param.12) | copy-start | bytes 49156
  7.2 100.4 %copy-start.4 = (f32[64,64]{1,0:T(8,128)S(1)}, f32[64,64]{1,0:T(8,128)}, u32[]{:S(2)}) copy-start(f32[64,64]{1,0:T(8,128)} %param.11) | copy-start | bytes 49156
  7.2 124.5 %all-gather.2.cloned.1.call-start = ((), (), s32[]{:S(2)}) async-start(), calls=%async_computation | async-start | bytes 4456448 | tf_op jit(solution)/shard_map/all_gather | solution.py:48
  107.6 17.9 %copy-start.2 = (f32[64,1024]{0,1:T(8,128)}, f32[64,1024]{0,1:T(8,128)S(1)}, u32[]{:S(2)}) copy-start(f32[64,1024]{0,1:T(8,128)S(1)} %all_gather.9) | copy-start | bytes 786436
  125.5 0.8 copy-start.1
Sparse Core Ops, SparseCore 0:
  9.9 44.4 all-gather.1
where the time goes:
time: 261 us; the launch traced here: 258 us
  blocking collectives  182 us (70%)
  matrix products  46.6 us (18%)
  between operations  14.3 us (5%)
  local copies, waits for them, and re-layouts  13.4 us (5%)
    psum x1, blocking collectives, local(): panel_sum, next_sum = lax.psum((earlier, next_part), 'col')  74.6 us
    psum x1, blocking collectives, local(): later = lax.psum(panel_part, 'col')  70.1 us
    dot_general x34, matrix products, contract(): lax.dot_general(left, right, (((1,), (1,)), ((), ())), precision=lax.Prec...  46.6 us
    all_gather x1, blocking collectives, local(): lax.all_gather(remaining, 'row', axis=1, tiled=True)  19.3 us
    all_gather x1, blocking collectives, local(): lax.all_gather(tile_inverse, 'row', axis=0, tiled=True)  17.9 us
    concatenate x11, local copies, waits for them, and re-layouts, solve_rows(): jnp.concatenate(pieces, axis=1)  8.32 us
  transfers between devices with their start and end apart: 1, of which 0 were waited for; matrix products, arithmetic and copies ran while one was open for 4% of the time, Pallas kernels for 0%

commit v1 on v0

v1 whole, which is shorter than its diff:
```python
import jax
import jax.numpy as jnp
from jax import lax
from jax.experimental import pallas as pl
from jax.experimental.pallas import tpu as pltpu
from jax.sharding import PartitionSpec as P

MESH = pl.DeviceIdType.MESH
TILE = 64
CHUNK = 1024
F32 = jnp.float32
BF16 = jnp.bfloat16


def nt(a, b):
    return lax.dot_general(a, b, (((1,), (1,)), ((), ())), preferred_element_type=F32)


def nn(a, b):
    return lax.dot_general(a, b, (((1,), (0,)), ((), ())), preferred_element_type=F32)


def parts(a):
    high = a.astype(BF16)
    return high, (a - high.astype(F32)).astype(BF16)


def product(a, b, dot):
    a_high, a_low = parts(a)
    b_high, b_low = parts(b)
    return dot(a_high, b_high) + (dot(a_high, b_low) + dot(a_low, b_high))


def pack(a):
    return jnp.concatenate([a[:32], a[32:]], axis=1)


def unpack(a):
    return jnp.concatenate([a[:, :64], a[:, 64:]], axis=0)


def unpack_pair(a, b):
    return jnp.concatenate(
        [
            jnp.concatenate([a[:, :64], b[:, :64]], axis=1),
            jnp.concatenate([a[:, 64:], b[:, 64:]], axis=1),
        ],
        axis=0,
    )


def kernel(
    factor_hbm,
    prior_hbm,
    lower_hbm,
    inverse_hbm,
    target_hbm,
    next_hbm,
    under_hbm,
    next_target_hbm,
    solution_ref,
    remainder_ref,
    factor,
    prior,
    nexts,
    lower,
    inverse,
    target,
    under,
    next_target,
    whole,
    panel_parts,
    next_parts,
    under_parts,
    reduced,
    load_sem,
    small_sem,
    col_send,
    col_recv,
    z_send,
    z_recv,
    pair_send,
    pair_recv,
    a_send,
    a_recv,
    b_send,
    b_recv,
    c_send,
    c_recv,
):
    r = lax.axis_index("row")
    c = lax.axis_index("col")
    z, core = r // 2, r % 2
    x, y = c // 4, c % 4
    quarter = (x + 2 * y) % 4
    sibling = (2 * z + 1 - core, c)
    chunks = factor.shape[1] // CHUNK

    small = []
    for i, (source, destination) in enumerate(
        (
            (lower_hbm, lower),
            (inverse_hbm, inverse),
            (under_hbm, under),
            (target_hbm, target),
            (next_target_hbm, next_target),
        )
    ):
        copy = pltpu.make_async_copy(source, destination, small_sem.at[i])
        copy.start()
        small.append(copy)

    def loads(i):
        at = pl.ds(pl.multiple_of(i * CHUNK, CHUNK), CHUNK)
        return [
            pltpu.make_async_copy(source.at[:, at], destination.at[:, at], load_sem.at[j, i])
            for j, (source, destination) in enumerate(
                ((prior_hbm, prior), (factor_hbm, factor), (next_hbm, nexts))
            )
        ]

    @pl.loop(0, chunks)
    def _(i):
        for copy in loads(i):
            copy.start()

    barrier = pltpu.get_barrier_semaphore()

    @pl.loop(1, 16)
    def _(k):
        pl.semaphore_signal(barrier, inc=1, device_id=(r, (c + k) % 16), device_id_type=MESH)

    @pl.loop(1, 8)
    def _(k):
        pl.semaphore_signal(
            barrier, inc=1, device_id=(2 * ((z + k) % 8) + core, c), device_id_type=MESH
        )

    pl.semaphore_signal(barrier, inc=1, device_id=sibling, device_id_type=MESH)

    for copy in small:
        copy.wait()
    own_rows = pl.ds(pl.multiple_of(r * TILE, TILE), TILE)
    whole[own_rows, :] = product(inverse[...], lower[...], nn)
    under_parts[c] = pack(under[...])

    def add(i, total):
        for copy in loads(i):
            copy.wait()
        at = pl.ds(pl.multiple_of(i * CHUNK, CHUNK), CHUNK)
        s_high, s_low = parts(prior[:, at])
        f_high, f_low = parts(factor[:, at])
        n_high, n_low = parts(nexts[:, at])
        return total + nt(
            jnp.concatenate([s_high, s_low], axis=0),
            jnp.concatenate([f_high, n_high, f_low, n_low], axis=0),
        )

    total = lax.fori_loop(0, chunks, add, jnp.zeros((128, 256), F32))
    sums = (total[:64, :128] + total[64:, 128:]) + (total[:64, 128:] + total[64:, :128])
    panel_parts[c] = pack(sums[:, :64])
    next_parts[c] = pack(sums[:, 64:])

    pl.semaphore_wait(barrier, 23)

    def over_col(buffer, i, k):
        return pltpu.make_async_remote_copy(
            src_ref=buffer.at[c],
            dst_ref=buffer.at[c],
            send_sem=col_send.at[i, k],
            recv_sem=col_recv.at[i, c],
            device_id=(r, (c + k) % 16),
            device_id_type=MESH,
        )

    def from_col(buffer, i, k):
        source = (c + k) % 16
        return pltpu.make_async_remote_copy(
            src_ref=buffer.at[source],
            dst_ref=buffer.at[source],
            send_sem=col_send.at[i, k],
            recv_sem=col_recv.at[i, source],
            device_id=(r, source),
            device_id_type=MESH,
        )

    @pl.loop(1, 16)
    def _(k):
        over_col(panel_parts, 0, k).start()

    def rows_of(tile, q, n, count=16):
        return whole.at[pl.ds(pl.multiple_of(tile * TILE + q * 16, 16), count), pl.ds(0, 128 * n)]

    def by_width(width, body):
        for n in range(1, 9):
            pl.when(width == n)(lambda n=n: body(n))

    def a_copy(n, k):
        return pltpu.make_async_remote_copy(
            src_ref=rows_of(r, quarter, n),
            dst_ref=rows_of(r, quarter, n),
            send_sem=a_send.at[k],
            recv_sem=a_recv.at[z],
            device_id=(2 * ((z + k) % 8) + core, c),
            device_id_type=MESH,
        )

    def c_copy(n, at, q, count):
        tile = 2 * at + core
        return pltpu.make_async_remote_copy(
            src_ref=rows_of(tile, q, n, count),
            dst_ref=rows_of(tile, q, n, count),
            send_sem=c_send.at[at, q],
            recv_sem=c_recv.at[at],
            device_id=sibling,
            device_id_type=MESH,
        )

    def distance(i):
        return (1 - i % 2) * (1 + i // 2) + (i % 2) * (7 - i // 2)

    def send_own(n):
        @pl.loop(0, 7)
        def _(i):
            a_copy(n, distance(i)).start()

        c_copy(n, z, 0, 64).start()

    by_width(z + core, send_own)

    @pl.loop(1, 16)
    def _(k):
        over_col(under_parts, 1, k).start()

    def b_copy(n, at, d, q):
        tile = 2 * at + core
        if d < 2:
            to = ((x + (1 if d == 0 else 3)) % 4) * 4 + y
        else:
            to = x * 4 + (y + 1 + 2 * (at % 2)) % 4
        return pltpu.make_async_remote_copy(
            src_ref=rows_of(tile, q, n),
            dst_ref=rows_of(tile, q, n),
            send_sem=b_send.at[d, at],
            recv_sem=b_recv.at[d, at],
            device_id=(r, to),
            device_id_type=MESH,
        )

    def a_wait(n, at):
        tile = 2 * at + core
        pltpu.make_async_remote_copy(
            src_ref=rows_of(tile, quarter, n),
            dst_ref=rows_of(tile, quarter, n),
            send_sem=a_send.at[0],
            recv_sem=a_recv.at[at],
            device_id=(tile, c),
            device_id_type=MESH,
        ).wait_recv()

    def forward(i, carry):
        at = (z + distance(i)) % 8

        def one(n):
            a_wait(n, at)
            for d in range(3):
                b_copy(n, at, d, quarter).start()
            c_copy(n, at, quarter, 16).start()

        by_width(at + core, one)
        return carry

    lax.fori_loop(0, 4, forward, 0)

    @pl.loop(1, 16)
    def _(k):
        from_col(panel_parts, 0, k).wait_recv()

    sum_1 = panel_parts[0]
    for k in range(1, 16):
        sum_1 = sum_1 + panel_parts[k]
    remaining = target[...] - unpack(sum_1)
    reduced[r] = pack(product(remaining, inverse[...], nt))

    def z_copy(k):
        return pltpu.make_async_remote_copy(
            src_ref=reduced.at[r],
            dst_ref=reduced.at[r],
            send_sem=z_send.at[k],
            recv_sem=z_recv.at[z],
            device_id=(2 * ((z + k) % 8) + core, c),
            device_id_type=MESH,
        )

    def pair_copy(at):
        return pltpu.make_async_remote_copy(
            src_ref=reduced.at[2 * at + core],
            dst_ref=reduced.at[2 * at + core],
            send_sem=pair_send.at[at],
            recv_sem=pair_recv.at[at],
            device_id=sibling,
            device_id_type=MESH,
        )

    @pl.loop(1, 8)
    def _(k):
        z_copy(k).start()

    pair_copy(z).start()

    lax.fori_loop(4, 7, forward, 0)

    @pl.loop(1, 16)
    def _(k):
        over_col(next_parts, 2, k).start()

    def others(i, carry):
        at = (z + distance(i)) % 8

        def one(n):
            for d, step in ((0, 3), (1, 1), (2, 2)):
                q = (quarter + step) % 4
                b_copy(n, at, d, q).wait_recv()
                c_copy(n, at, q, 16).start()

        by_width(at + core, one)
        return carry

    lax.fori_loop(0, 7, others, 0)

    @pl.loop(0, 7)
    def _(i):
        at = (z + distance(i)) % 8
        pltpu.make_async_remote_copy(
            src_ref=reduced.at[2 * at + core],
            dst_ref=reduced.at[2 * at + core],
            send_sem=z_send.at[0],
            recv_sem=z_recv.at[at],
            device_id=(2 * at + core, c),
            device_id_type=MESH,
        ).wait_recv()
        pair_copy(at).start()

    @pl.loop(1, 16)
    def _(k):
        from_col(under_parts, 1, k).wait_recv()

    @pl.loop(1, 16)
    def _(k):
        from_col(next_parts, 2, k).wait_recv()

    @pl.loop(0, 8)
    def _(at):
        tile = 2 * at + 1 - core

        def one(n):
            pltpu.make_async_remote_copy(
                src_ref=rows_of(tile, 0, n, 64),
                dst_ref=rows_of(tile, 0, n, 64),
                send_sem=c_send.at[at, 0],
                recv_sem=c_recv.at[at],
                device_id=sibling,
                device_id_type=MESH,
            ).wait_recv()

        by_width(at + 1 - core, one)
        pltpu.make_async_remote_copy(
            src_ref=reduced.at[tile],
            dst_ref=reduced.at[tile],
            send_sem=pair_send.at[at],
            recv_sem=pair_recv.at[at],
            device_id=sibling,
            device_id_type=MESH,
        ).wait_recv()

    @pl.loop(1, 16)
    def _(k):
        over_col(panel_parts, 0, k).wait_send()
        over_col(under_parts, 1, k).wait_send()
        over_col(next_parts, 2, k).wait_send()

    @pl.loop(1, 8)
    def _(k):
        z_copy(k).wait_send()

    @pl.loop(0, 8)
    def _(at):
        pair_copy(at).wait_send()

    def own_sent(n):
        @pl.loop(1, 8)
        def _(k):
            a_copy(n, k).wait_send()

        c_copy(n, z, 0, 64).wait_send()

    by_width(z + core, own_sent)

    @pl.loop(0, 7)
    def _(i):
        at = (z + distance(i)) % 8

        def one(n):
            for d in range(3):
                b_copy(n, at, d, quarter).wait_send()
            for q in range(4):
                c_copy(n, at, q, 16).wait_send()

        by_width(at + core, one)

    held = []
    for p in range(8):
        right = unpack_pair(reduced[2 * p], reduced[2 * p + 1])
        link = whole[128 * p + 64 : 128 * p + 128, 128 * p : 128 * p + 128]
        link = link[:, :64]
        held.append(
            jnp.concatenate(
                [right[:, :64], right[:, 64:] - product(right[:, :64], link, nt)], axis=1
            )
        )
        if p > 0:
            even = whole[128 * p : 128 * p + 64, : 128 * p]
            odd = whole[128 * p + 64 : 128 * p + 128, : 128 * p]
            whole[128 * p + 64 : 128 * p + 128, : 128 * p] = odd - product(link, even, nn)

    later = jnp.zeros((64, 64), F32)
    for p in range(8):
        solved = held[p]
        reduced[2 * p] = solved[:32]
        reduced[2 * p + 1] = solved[32:]
        if p < 7:
            change = product(
                solved, whole[128 * (p + 1) :, 128 * p : 128 * (p + 1)], nt
            )
            for m in range(p + 1, 8):
                at = 128 * (m - p - 1)
                held[m] = held[m] - change[:, at : at + 128]
        later = later + product(
            solved, unpack_pair(under_parts[2 * p], under_parts[2 * p + 1]), nt
        )

    mine = jnp.concatenate([reduced[2 * z], reduced[2 * z + 1]], axis=0)
    solution_ref[...] = jnp.where(core == 0, mine[:, :64], mine[:, 64:])
    sum_2 = next_parts[0]
    for k in range(1, 16):
        sum_2 = sum_2 + next_parts[k]
    remainder_ref[...] = next_target[...] - unpack(sum_2) - later


def local(*args):
    factor, prior, lower, inverse, target = args[:5]
    width = factor.shape[1]
    out = jax.ShapeDtypeStruct(target.shape, F32)
    return pl.pallas_call(
        kernel,
        out_shape=(out, out),
        in_specs=[pl.BlockSpec(memory_space=pltpu.HBM)] * 8,
        out_specs=(pl.BlockSpec(memory_space=pltpu.VMEM),) * 2,
        scratch_shapes=[
            pltpu.VMEM((64, width), F32),
            pltpu.VMEM((64, width), F32),
            pltpu.VMEM((64, width), F32),
            pltpu.VMEM((64, 1024), F32),
            pltpu.VMEM((64, 64), F32),
            pltpu.VMEM((64, 64), F32),
            pltpu.VMEM((64, 64), F32),
            pltpu.VMEM((64, 64), F32),
            pltpu.VMEM((1024, 1024), F32),
            pltpu.VMEM((16, 32, 128), F32),
            pltpu.VMEM((16, 32, 128), F32),
            pltpu.VMEM((16, 32, 128), F32),
            pltpu.VMEM((16, 32, 128), F32),
            pltpu.SemaphoreType.DMA((3, width // CHUNK)),
            pltpu.SemaphoreType.DMA((5,)),
            pltpu.SemaphoreType.DMA((3, 16)),
            pltpu.SemaphoreType.DMA((3, 16)),
            pltpu.SemaphoreType.DMA((8,)),
            pltpu.SemaphoreType.DMA((8,)),
            pltpu.SemaphoreType.DMA((8,)),
            pltpu.SemaphoreType.DMA((8,)),
            pltpu.SemaphoreType.DMA((8,)),
            pltpu.SemaphoreType.DMA((8,)),
            pltpu.SemaphoreType.DMA((3, 8)),
            pltpu.SemaphoreType.DMA((3, 8)),
            pltpu.SemaphoreType.DMA((8, 4)),
            pltpu.SemaphoreType.DMA((8,)),
        ],
        compiler_params=pltpu.CompilerParams(
            collective_id=0, has_side_effects=True, vmem_limit_bytes=60 * 1024 * 1024
        ),
    )(*args)


def solution(mesh):
    return jax.shard_map(
        local,
        mesh=mesh,
        in_specs=(
            P("row", "col"),
            P(None, "col"),
            P("row", None),
            P("row", None),
            P(None, "row"),
            P("row", "col"),
            P("row", "col"),
            P(None, "row"),
        ),
        out_specs=(P(None, "row"), P(None, "row")),
        check_vma=False,
    )
```

time: 261 us -> 42 us (0.16)
  the two profiles are of different devices: /device:TPU:32 before, /device:TPU:64 now
where the time goes in v1:
time: 42 us; the launch traced here: 41.8 us
  Pallas kernels  38.4 us (91%)
  local copies, waits for them, and re-layouts  2.75 us (7%)
  between operations  0.64 us (2%)
    pallas_call x1, Pallas kernels, local(): pl.pallas_call(kernel, out_shape=(out, out), in_specs=[pl.BlockSpec(memor...  38.4 us
    unnamed x2, local copies, waits for them, and re-layouts  2.75 us

profile of v1, /device:TPU:64, one launch (start us, length us, event | category | flops | bytes accessed | tf_op | source)
XLA Modules:
  0.0 41.8 jit_solution(5915881233583202841)
XLA Ops:
  0.6 38.4 %shard_map.95 = (f32[64,64]{1,0:T(8,128)}, f32[64,64]{1,0:T(8,128)}) custom-call(f32[64,12288]{1,0:T(8,128)} %factor_hbm.1, f32[64,12288]{1,0:T(8,128)} %prior_hbm.1, f32[64,1024]{1,0:T(8,128)} %lower_hbm.1, f32[64,64]{1,0:T(8,128)} %inverse_hbm.1, f32[64,64]{1,0:T(8,128)} %target_hbm.1, f32[64,12288]{1,0:T(8,128)} %next_hbm.1, f32[64,64]{1,0:T(8,128)} %under_hbm.1, ...), custom_call_target="tpu_custom_call" | custom-call | tf_op jit(solution)/shard_map/pallas_call | solution.py:454
  39.0 1.4 %copy.12 = f32[64,64]{1,0:T(8,128)} copy(f32[64,64]{1,0:T(8,128)} %get-tuple-element.4) | data formatting | bytes 32768
  40.4 1.4 %copy.13 = f32[64,64]{1,0:T(8,128)} copy(f32[64,64]{1,0:T(8,128)} %get-tuple-element.5) | data formatting | bytes 32768

commit v2 on v1

v2 whole, which is shorter than its diff:
```python
import jax
import jax.numpy as jnp
from jax import lax
from jax.experimental import pallas as pl
from jax.experimental.pallas import tpu as pltpu
from jax.sharding import PartitionSpec as P

MESH = pl.DeviceIdType.MESH
TILE = 64
CHUNK = 2048
F32 = jnp.float32
BF16 = jnp.bfloat16


def nt(a, b):
    return lax.dot_general(a, b, (((1,), (1,)), ((), ())), preferred_element_type=F32)


def nn(a, b):
    return lax.dot_general(a, b, (((1,), (0,)), ((), ())), preferred_element_type=F32)


def parts(a):
    high = a.astype(BF16)
    return high, (a - high.astype(F32)).astype(BF16)


def product(a, b, dot):
    a_high, a_low = parts(a)
    b_high, b_low = parts(b)
    return dot(a_high, b_high) + (dot(a_high, b_low) + dot(a_low, b_high))


def pack(a):
    return jnp.concatenate([a[:32], a[32:]], axis=1)


def unpack(a):
    return jnp.concatenate([a[:, :64], a[:, 64:]], axis=0)


def unpack_pair(a, b):
    return jnp.concatenate(
        [
            jnp.concatenate([a[:, :64], b[:, :64]], axis=1),
            jnp.concatenate([a[:, 64:], b[:, 64:]], axis=1),
        ],
        axis=0,
    )


def kernel(
    factor_hbm,
    prior_hbm,
    lower_hbm,
    inverse_hbm,
    target_hbm,
    next_hbm,
    under_hbm,
    next_target_hbm,
    out_ref,
    prior,
    lower,
    small,
    whole,
    panel_parts,
    next_parts,
    under_parts,
    reduced,
    load_sem,
    small_sem,
    col_send,
    col_recv,
    z_sem,
    pair_sem,
    a_send,
    a_recv,
    b_send,
    b_recv,
    c_send,
    c_recv,
):
    r = lax.axis_index("row")
    c = lax.axis_index("col")
    z, core = r // 2, r % 2
    x, y = c // 4, c % 4
    quarter = (x + 2 * y) % 4
    sibling = (2 * z + 1 - core, c)
    chunks = prior.shape[1] // CHUNK

    pltpu.make_async_copy(lower_hbm, lower, small_sem.at[0]).start()
    for i, source in enumerate((inverse_hbm, under_hbm, target_hbm, next_target_hbm)):
        pltpu.make_async_copy(source, small.at[i], small_sem.at[1]).start()

    def columns(i):
        return pl.ds(pl.multiple_of(i * CHUNK, CHUNK), CHUNK)

    @pl.loop(0, chunks)
    def _(i):
        for j, source in enumerate((prior_hbm, factor_hbm, next_hbm)):
            pltpu.make_async_copy(
                source.at[:, columns(i)],
                prior.at[pl.ds(TILE * j, TILE), columns(i)],
                load_sem.at[i],
            ).start()

    barrier = pltpu.get_barrier_semaphore()

    @pl.loop(1, 16)
    def _(k):
        pl.semaphore_signal(barrier, inc=1, device_id=(r, (c + k) % 16), device_id_type=MESH)

    @pl.loop(1, 8)
    def _(k):
        pl.semaphore_signal(
            barrier, inc=1, device_id=(2 * ((z + k) % 8) + core, c), device_id_type=MESH
        )

    pl.semaphore_signal(barrier, inc=1, device_id=sibling, device_id_type=MESH)

    pltpu.make_async_copy(lower, lower, small_sem.at[0]).wait()
    pltpu.make_async_copy(small, small, small_sem.at[1]).wait()
    inverse, target, next_target = small.at[0], small.at[2], small.at[3]
    own_rows = pl.ds(pl.multiple_of(r * TILE, TILE), TILE)
    whole[own_rows, :] = product(inverse[...], lower[...], nn)
    under_parts[c] = pack(small[1])

    pl.semaphore_wait(barrier, 23)

    def over_col(buffer, i, k):
        return pltpu.make_async_remote_copy(
            src_ref=buffer.at[c],
            dst_ref=buffer.at[c],
            send_sem=col_send.at[i],
            recv_sem=col_recv.at[i],
            device_id=(r, (c + k) % 16),
            device_id_type=MESH,
        )

    def all_col(buffer, i):
        return pltpu.make_async_remote_copy(
            src_ref=buffer.at[pl.ds(0, 15)],
            dst_ref=buffer.at[pl.ds(0, 15)],
            send_sem=col_send.at[i],
            recv_sem=col_recv.at[i],
            device_id=(r, (c + 1) % 16),
            device_id_type=MESH,
        )

    def rows_of(tile, q, n, count=16):
        return whole.at[pl.ds(pl.multiple_of(tile * TILE + q * 16, 16), count), pl.ds(0, 128 * n)]

    def by_width(width, body):
        for n in range(1, 9):
            pl.when(width == n)(lambda n=n: body(n))

    def a_copy(n, k):
        return pltpu.make_async_remote_copy(
            src_ref=rows_of(r, quarter, n),
            dst_ref=rows_of(r, quarter, n),
            send_sem=a_send.at[0],
            recv_sem=a_recv.at[z],
            device_id=(2 * ((z + k) % 8) + core, c),
            device_id_type=MESH,
        )

    def c_copy(n, at, q, count):
        tile = 2 * at + core
        return pltpu.make_async_remote_copy(
            src_ref=rows_of(tile, q, n, count),
            dst_ref=rows_of(tile, q, n, count),
            send_sem=c_send.at[at],
            recv_sem=c_recv.at[at],
            device_id=sibling,
            device_id_type=MESH,
        )

    def distance(i):
        return (1 - i % 2) * (1 + i // 2) + (i % 2) * (7 - i // 2)

    def send_own(n):
        @pl.loop(0, 7)
        def _(i):
            a_copy(n, distance(i)).start()

        c_copy(n, z, 0, 64).start()

    by_width(z + core, send_own)

    def add(i, total):
        at = columns(i)
        pltpu.make_async_copy(prior.at[:, at], prior.at[:, at], load_sem.at[i]).wait()
        s_high, s_low = parts(prior[:TILE, at])
        f_high, f_low = parts(prior[TILE:, at])
        return total + nt(
            jnp.concatenate([s_high, s_low], axis=0), jnp.concatenate([f_high, f_low], axis=0)
        )

    total = lax.fori_loop(0, chunks, add, jnp.zeros((128, 256), F32))
    sums = (total[:64, :128] + total[64:, 128:]) + (total[:64, 128:] + total[64:, :128])
    panel_parts[c] = pack(sums[:, :64])

    @pl.loop(1, 16)
    def _(k):
        over_col(panel_parts, 0, k).start()

    next_parts[c] = pack(sums[:, 64:])

    @pl.loop(1, 16)
    def _(k):
        over_col(under_parts, 1, k).start()

    def b_copy(n, at, d, q):
        tile = 2 * at + core
        if d < 2:
            to = ((x + (1 if d == 0 else 3)) % 4) * 4 + y
        else:
            to = x * 4 + (y + 1 + 2 * (at % 2)) % 4
        return pltpu.make_async_remote_copy(
            src_ref=rows_of(tile, q, n),
            dst_ref=rows_of(tile, q, n),
            send_sem=b_send.at[at],
            recv_sem=b_recv.at[at],
            device_id=(r, to),
            device_id_type=MESH,
        )

    def b_all(n, at):
        return pltpu.make_async_remote_copy(
            src_ref=whole.at[pl.ds(0, 48), pl.ds(0, 128 * n)],
            dst_ref=whole.at[pl.ds(0, 48), pl.ds(0, 128 * n)],
            send_sem=b_send.at[at],
            recv_sem=b_recv.at[at],
            device_id=(r, (c + 1) % 16),
            device_id_type=MESH,
        )

    def a_wait(n, at):
        tile = 2 * at + core
        pltpu.make_async_remote_copy(
            src_ref=rows_of(tile, quarter, n),
            dst_ref=rows_of(tile, quarter, n),
            send_sem=a_send.at[0],
            recv_sem=a_recv.at[at],
            device_id=(tile, c),
            device_id_type=MESH,
        ).wait_recv()

    def forward(i, carry):
        at = (z + distance(i)) % 8

        def one(n):
            a_wait(n, at)
            for d in range(3):
                b_copy(n, at, d, quarter).start()
            c_copy(n, at, quarter, 16).start()

        by_width(at + core, one)
        return carry

    lax.fori_loop(0, 4, forward, 0)

    all_col(panel_parts, 0).wait_recv()
    sum_1 = panel_parts[0]
    for k in range(1, 16):
        sum_1 = sum_1 + panel_parts[k]
    remaining = target[...] - unpack(sum_1)
    reduced[core, z] = pack(product(remaining, inverse[...], nt))

    def z_copy(k):
        return pltpu.make_async_remote_copy(
            src_ref=reduced.at[core, z],
            dst_ref=reduced.at[core, z],
            send_sem=z_sem.at[0],
            recv_sem=z_sem.at[1],
            device_id=(2 * ((z + k) % 8) + core, c),
            device_id_type=MESH,
        )

    all_z = pltpu.make_async_remote_copy(
        src_ref=reduced.at[core, pl.ds(0, 7)],
        dst_ref=reduced.at[core, pl.ds(0, 7)],
        send_sem=z_sem.at[0],
        recv_sem=z_sem.at[1],
        device_id=(2 * ((z + 1) % 8) + core, c),
        device_id_type=MESH,
    )
    pair = pltpu.make_async_remote_copy(
        src_ref=reduced.at[core],
        dst_ref=reduced.at[core],
        send_sem=pair_sem.at[0],
        recv_sem=pair_sem.at[1],
        device_id=sibling,
        device_id_type=MESH,
    )

    @pl.loop(1, 8)
    def _(k):
        z_copy(k).start()

    lax.fori_loop(4, 7, forward, 0)

    @pl.loop(1, 16)
    def _(k):
        over_col(next_parts, 2, k).start()

    def others(i, carry):
        at = (z + distance(i)) % 8

        def one(n):
            b_all(n, at).wait_recv()
            for step in range(1, 4):
                c_copy(n, at, (quarter + step) % 4, 16).start()

        by_width(at + core, one)
        return carry

    lax.fori_loop(0, 7, others, 0)

    all_z.wait_recv()
    pair.start()
    all_col(under_parts, 1).wait_recv()
    all_col(next_parts, 2).wait_recv()

    @pl.loop(0, 8)
    def _(at):
        def one(n):
            tile = 2 * at + 1 - core
            pltpu.make_async_remote_copy(
                src_ref=rows_of(tile, 0, n, 64),
                dst_ref=rows_of(tile, 0, n, 64),
                send_sem=c_send.at[at],
                recv_sem=c_recv.at[at],
                device_id=sibling,
                device_id_type=MESH,
            ).wait_recv()

        by_width(at + 1 - core, one)

    pair.wait_recv()

    for i, buffer in enumerate((panel_parts, under_parts, next_parts)):
        all_col(buffer, i).wait_send()
    all_z.wait_send()
    pair.wait_send()

    def own_sent(n):
        pltpu.make_async_remote_copy(
            src_ref=whole.at[pl.ds(0, 112), pl.ds(0, 128 * n)],
            dst_ref=whole.at[pl.ds(0, 112), pl.ds(0, 128 * n)],
            send_sem=a_send.at[0],
            recv_sem=a_recv.at[0],
            device_id=sibling,
            device_id_type=MESH,
        ).wait_send()

    by_width(z + core, own_sent)

    @pl.loop(0, 8)
    def _(at):
        def one(n):
            c_copy(n, at, 0, 64).wait_send()

            @pl.when(at != z)
            def _():
                b_all(n, at).wait_send()

        by_width(at + core, one)

    held = []
    for p in range(8):
        right = unpack_pair(reduced[0, p], reduced[1, p])
        link = whole[128 * p + 64 : 128 * p + 128, 128 * p : 128 * p + 128]
        link = link[:, :64]
        held.append(
            jnp.concatenate(
                [right[:, :64], right[:, 64:] - product(right[:, :64], link, nt)], axis=1
            )
        )
        if p > 0:
            even = whole[128 * p : 128 * p + 64, : 128 * p]
            odd = whole[128 * p + 64 : 128 * p + 128, : 128 * p]
            whole[128 * p + 64 : 128 * p + 128, : 128 * p] = odd - product(link, even, nn)

    later = jnp.zeros((64, 64), F32)
    for p in range(8):
        solved = held[p]
        reduced[0, p] = solved[:32]
        reduced[1, p] = solved[32:]
        if p < 7:
            change = product(
                solved, whole[128 * (p + 1) :, 128 * p : 128 * (p + 1)], nt
            )
            for m in range(p + 1, 8):
                at = 128 * (m - p - 1)
                held[m] = held[m] - change[:, at : at + 128]
        later = later + product(
            solved, unpack_pair(under_parts[2 * p], under_parts[2 * p + 1]), nt
        )

    mine = jnp.concatenate([reduced[0, z], reduced[1, z]], axis=0)
    own = jnp.where(core == 0, mine[:, :64], mine[:, 64:])
    sum_2 = next_parts[0]
    for k in range(1, 16):
        sum_2 = sum_2 + next_parts[k]
    remainder = next_target[...] - unpack(sum_2) - later
    out_ref[...] = jnp.concatenate([own, remainder], axis=1)


def local(*args):
    width = args[0].shape[1]
    chunks = width // CHUNK
    dma = pltpu.SemaphoreType.DMA
    out = pl.pallas_call(
        kernel,
        out_shape=jax.ShapeDtypeStruct((64, 128), F32),
        in_specs=[pl.BlockSpec(memory_space=pltpu.HBM)] * 8,
        out_specs=pl.BlockSpec(memory_space=pltpu.VMEM),
        scratch_shapes=[
            pltpu.VMEM((192, width), F32),
            pltpu.VMEM((64, 1024), F32),
            pltpu.VMEM((4, 64, 64), F32),
            pltpu.VMEM((1024, 1024), F32),
            pltpu.VMEM((16, 32, 128), F32),
            pltpu.VMEM((16, 32, 128), F32),
            pltpu.VMEM((16, 32, 128), F32),
            pltpu.VMEM((2, 8, 32, 128), F32),
            dma((chunks,)),
            dma((2,)),
            dma((3,)),
            dma((3,)),
            dma((2,)),
            dma((2,)),
            dma((1,)),
            dma((8,)),
            dma((8,)),
            dma((8,)),
            dma((8,)),
            dma((8,)),
        ],
        compiler_params=pltpu.CompilerParams(
            collective_id=0, has_side_effects=True, vmem_limit_bytes=60 * 1024 * 1024
        ),
    )(*args)
    return out[:, :64], out[:, 64:]


def solution(mesh):
    return jax.shard_map(
        local,
        mesh=mesh,
        in_specs=(
            P("row", "col"),
            P(None, "col"),
            P("row", None),
            P("row", None),
            P(None, "row"),
            P("row", "col"),
            P("row", "col"),
            P(None, "row"),
        ),
        out_specs=(P(None, "row"), P(None, "row")),
        check_vma=False,
    )
```

time: 42 us -> 36.8 us (0.88)
  the two profiles are of different devices: /device:TPU:64 before, /device:TPU:1 now
where the time goes in v2:
time: 36.8 us; the launch traced here: 36.7 us
  Pallas kernels  34.5 us (94%)
  local copies, waits for them, and re-layouts  1.53 us (4%)
  between operations  0.64 us (2%)
    pallas_call x1, Pallas kernels, local(): pl.pallas_call(kernel, out_shape=jax.ShapeDtypeStruct((64, 128), F32), in...  34.5 us
    slice x1, local copies, waits for them, and re-layouts, local(): return (out[:, :64], out[:, 64:])  1.53 us

profile of v2, /device:TPU:1, one launch (start us, length us, event | category | flops | bytes accessed | tf_op | source)
XLA Modules:
  0.0 36.7 jit_solution(11495413044028645680)
XLA Ops:
  0.6 34.5 %shard_map.95 = f32[64,128]{1,0:T(8,128)} custom-call(f32[64,12288]{1,0:T(8,128)} %factor_hbm.1, f32[64,12288]{1,0:T(8,128)} %prior_hbm.1, f32[64,1024]{1,0:T(8,128)} %lower_hbm.1, f32[64,64]{1,0:T(8,128)} %inverse_hbm.1, f32[64,64]{1,0:T(8,128)} %target_hbm.1, f32[64,12288]{1,0:T(8,128)} %next_hbm.1, f32[64,64]{1,0:T(8,128)} %under_hbm.1, ...), custom_call_target="tpu_custom_call" | custom-call | tf_op jit(solution)/shard_map/pallas_call | solution.py:414
  35.1 1.5 %fusion = (f32[64,64]{1,0:T(8,128)}, f32[64,64]{1,0:T(8,128)}) fusion(f32[64,128]{1,0:T(8,128)} %shard_map.95), kind=kLoop, calls=%fused_computation | loop fusion | bytes 65536 | tf_op jit(solution)/shard_map/slice | solution.py:445

commit v3 on v2

v3 whole, which is shorter than its diff:
```python
import jax
import jax.numpy as jnp
from jax import lax
from jax.experimental import pallas as pl
from jax.experimental.pallas import tpu as pltpu
from jax.sharding import PartitionSpec as P

MESH = pl.DeviceIdType.MESH
TILE = 64
CHUNK = 2048
F32 = jnp.float32
BF16 = jnp.bfloat16


def nt(a, b):
    return lax.dot_general(a, b, (((1,), (1,)), ((), ())), preferred_element_type=F32)


def nn(a, b):
    return lax.dot_general(a, b, (((1,), (0,)), ((), ())), preferred_element_type=F32)


def parts(a):
    high = a.astype(BF16)
    return high, (a - high.astype(F32)).astype(BF16)


def product(a, b, dot):
    a_high, a_low = parts(a)
    b_high, b_low = parts(b)
    return dot(a_high, b_high) + (dot(a_high, b_low) + dot(a_low, b_high))


def pack(a):
    return jnp.concatenate([a[:32], a[32:]], axis=1)


def unpack(a):
    return jnp.concatenate([a[:, :64], a[:, 64:]], axis=0)


def unpack_pair(a, b):
    return jnp.concatenate(
        [
            jnp.concatenate([a[:, :64], b[:, :64]], axis=1),
            jnp.concatenate([a[:, 64:], b[:, 64:]], axis=1),
        ],
        axis=0,
    )


def kernel(
    factor_hbm,
    prior_hbm,
    lower_hbm,
    inverse_hbm,
    target_hbm,
    next_hbm,
    under_hbm,
    next_target_hbm,
    out_ref,
    prior,
    lower,
    small,
    whole,
    whole_high,
    whole_low,
    under_high,
    under_low,
    solved,
    panel_parts,
    next_parts,
    under_parts,
    reduced,
    load_sem,
    small_sem,
    col_send,
    col_recv,
    z_send,
    z_recv,
    pair_send,
    pair_recv,
    a_send,
    a_recv,
    b_send,
    b_recv,
    c_send,
    c_recv,
):
    r = lax.axis_index("row")
    c = lax.axis_index("col")
    z, core = r // 2, r % 2
    x, y = c // 4, c % 4
    quarter = (x + 2 * y) % 4
    sibling = (2 * z + 1 - core, c)
    chunks = prior.shape[1] // CHUNK

    pltpu.make_async_copy(lower_hbm, lower, small_sem.at[0]).start()
    for i, source in enumerate((inverse_hbm, under_hbm, target_hbm, next_target_hbm)):
        pltpu.make_async_copy(source, small.at[i], small_sem.at[1]).start()

    def columns(i):
        return pl.ds(pl.multiple_of(i * CHUNK, CHUNK), CHUNK)

    @pl.loop(0, chunks)
    def _(i):
        for j, source in enumerate((prior_hbm, factor_hbm, next_hbm)):
            pltpu.make_async_copy(
                source.at[:, columns(i)],
                prior.at[pl.ds(TILE * j, TILE), columns(i)],
                load_sem.at[i],
            ).start()

    barrier = pltpu.get_barrier_semaphore()

    @pl.loop(1, 16)
    def _(k):
        pl.semaphore_signal(barrier, inc=1, device_id=(r, (c + k) % 16), device_id_type=MESH)

    @pl.loop(1, 8)
    def _(k):
        pl.semaphore_signal(
            barrier, inc=1, device_id=(2 * ((z + k) % 8) + core, c), device_id_type=MESH
        )

    pl.semaphore_signal(barrier, inc=1, device_id=sibling, device_id_type=MESH)

    pltpu.make_async_copy(lower, lower, small_sem.at[0]).wait()
    pltpu.make_async_copy(small, small, small_sem.at[1]).wait()
    inverse, target, next_target = small.at[0], small.at[2], small.at[3]
    own_rows = pl.ds(pl.multiple_of(r * TILE, TILE), TILE)
    whole[own_rows, :] = product(inverse[...], lower[...], nn)
    under_parts[c] = pack(small[1])

    def add(i, total):
        at = columns(i)
        pltpu.make_async_copy(prior.at[:, at], prior.at[:, at], load_sem.at[i]).wait()
        s_high, s_low = parts(prior[:TILE, at])
        f_high, f_low = parts(prior[TILE:, at])
        return total + nt(
            jnp.concatenate([s_high, s_low], axis=0), jnp.concatenate([f_high, f_low], axis=0)
        )

    total = lax.fori_loop(0, 2, add, jnp.zeros((128, 256), F32))
    pl.semaphore_wait(barrier, 23)

    def over_col(buffer, i, k):
        return pltpu.make_async_remote_copy(
            src_ref=buffer.at[c],
            dst_ref=buffer.at[c],
            send_sem=col_send.at[i],
            recv_sem=col_recv.at[i],
            device_id=(r, (c + k) % 16),
            device_id_type=MESH,
        )

    def all_col(buffer, i):
        return pltpu.make_async_remote_copy(
            src_ref=buffer.at[pl.ds(0, 15)],
            dst_ref=buffer.at[pl.ds(0, 15)],
            send_sem=col_send.at[i],
            recv_sem=col_recv.at[i],
            device_id=(r, (c + 1) % 16),
            device_id_type=MESH,
        )

    def rows_of(tile, q, n, count=16):
        return whole.at[pl.ds(pl.multiple_of(tile * TILE + q * 16, 16), count), pl.ds(0, 128 * n)]

    def by_width(width, body):
        for n in range(1, 9):
            pl.when(width == n)(lambda n=n: body(n))

    def a_copy(n, k):
        return pltpu.make_async_remote_copy(
            src_ref=rows_of(r, quarter, n),
            dst_ref=rows_of(r, quarter, n),
            send_sem=a_send.at[0],
            recv_sem=a_recv.at[z],
            device_id=(2 * ((z + k) % 8) + core, c),
            device_id_type=MESH,
        )

    def c_copy(n, at, q, count):
        tile = 2 * at + core
        return pltpu.make_async_remote_copy(
            src_ref=rows_of(tile, q, n, count),
            dst_ref=rows_of(tile, q, n, count),
            send_sem=c_send.at[at],
            recv_sem=c_recv.at[at],
            device_id=sibling,
            device_id_type=MESH,
        )

    def send_own(n):
        @pl.loop(1, 8)
        def _(k):
            a_copy(n, k).start()

        c_copy(n, z, 0, 64).start()

    by_width(z + core, send_own)

    @pl.loop(1, 16)
    def _(k):
        over_col(under_parts, 1, k).start()

    total = lax.fori_loop(2, chunks, add, total)
    sums = (total[:64, :128] + total[64:, 128:]) + (total[:64, 128:] + total[64:, :128])
    panel_parts[c] = pack(sums[:, :64])

    @pl.loop(1, 16)
    def _(k):
        over_col(panel_parts, 0, k).start()

    next_parts[c] = pack(sums[:, 64:])

    def b_copy(n, at, d, q):
        tile = 2 * at + core
        if d < 2:
            to = ((x + (1 if d == 0 else 3)) % 4) * 4 + y
        else:
            to = x * 4 + (y + 1 + 2 * (at % 2)) % 4
        return pltpu.make_async_remote_copy(
            src_ref=rows_of(tile, q, n),
            dst_ref=rows_of(tile, q, n),
            send_sem=b_send.at[at],
            recv_sem=b_recv.at[at],
            device_id=(r, to),
            device_id_type=MESH,
        )

    def b_all(n, at):
        return pltpu.make_async_remote_copy(
            src_ref=whole.at[pl.ds(0, 48), pl.ds(0, 128 * n)],
            dst_ref=whole.at[pl.ds(0, 48), pl.ds(0, 128 * n)],
            send_sem=b_send.at[at],
            recv_sem=b_recv.at[at],
            device_id=(r, (c + 1) % 16),
            device_id_type=MESH,
        )

    def a_wait(n, at):
        tile = 2 * at + core
        pltpu.make_async_remote_copy(
            src_ref=rows_of(tile, quarter, n),
            dst_ref=rows_of(tile, quarter, n),
            send_sem=a_send.at[0],
            recv_sem=a_recv.at[at],
            device_id=(tile, c),
            device_id_type=MESH,
        ).wait_recv()

    def forward(half):
        @pl.loop(4 * half, 4 * half + 4)
        def _(at):
            def one(n):
                a_wait(n, at)
                for d in range(3):
                    b_copy(n, at, d, quarter).start()
                c_copy(n, at, quarter, 16).start()

            pl.when(at != z)(lambda: by_width(at + core, one))

    forward(0)
    pl.when(z >= 4)(lambda: forward(1))

    all_col(panel_parts, 0).wait_recv()
    sum_1 = panel_parts[0]
    for k in range(1, 16):
        sum_1 = sum_1 + panel_parts[k]
    remaining = target[...] - unpack(sum_1)
    reduced[core, z] = pack(product(remaining, inverse[...], nt))

    def z_copy(k):
        return pltpu.make_async_remote_copy(
            src_ref=reduced.at[core, z],
            dst_ref=reduced.at[core, z],
            send_sem=z_send.at[0],
            recv_sem=z_recv.at[z // 4],
            device_id=(2 * ((z + k) % 8) + core, c),
            device_id_type=MESH,
        )

    def z_all(count, half):
        return pltpu.make_async_remote_copy(
            src_ref=reduced.at[core, pl.ds(0, count)],
            dst_ref=reduced.at[core, pl.ds(0, count)],
            send_sem=z_send.at[0],
            recv_sem=z_recv.at[half],
            device_id=(2 * ((z + 1) % 8) + core, c),
            device_id_type=MESH,
        )

    def pair(half):
        return pltpu.make_async_remote_copy(
            src_ref=reduced.at[core, pl.ds(4 * half, 4)],
            dst_ref=reduced.at[core, pl.ds(4 * half, 4)],
            send_sem=pair_send.at[half],
            recv_sem=pair_recv.at[half],
            device_id=sibling,
            device_id_type=MESH,
        )

    @pl.loop(1, 8)
    def _(k):
        z_copy(k).start()

    pl.when(z < 4)(lambda: forward(1))

    @pl.loop(1, 16)
    def _(k):
        over_col(next_parts, 2, k).start()

    def others(half):
        @pl.loop(4 * half, 4 * half + 4)
        def _(at):
            def one(n):
                b_all(n, at).wait_recv()
                for step in range(1, 4):
                    c_copy(n, at, (quarter + step) % 4, 16).start()

            pl.when(at != z)(lambda: by_width(at + core, one))

    def to_sibling(half):
        pl.when(z // 4 == half)(lambda: z_all(3, half).wait_recv())
        pl.when(z // 4 != half)(lambda: z_all(4, half).wait_recv())
        pair(half).start()

    def from_sibling(half):
        @pl.loop(4 * half, 4 * half + 4)
        def _(at):
            def one(n):
                tile = 2 * at + 1 - core
                pltpu.make_async_remote_copy(
                    src_ref=rows_of(tile, 0, n, 64),
                    dst_ref=rows_of(tile, 0, n, 64),
                    send_sem=c_send.at[at],
                    recv_sem=c_recv.at[at],
                    device_id=sibling,
                    device_id_type=MESH,
                ).wait_recv()

            by_width(at + 1 - core, one)

    def prepare(half):
        links = []
        for p in range(4 * half, 4 * half + 4):
            even = slice(128 * p, 128 * p + 64)
            odd = slice(128 * p + 64, 128 * p + 128)
            link = parts(whole[odd, 128 * p : 128 * p + 128][:, :64])
            links.append(link)
            if p > 0:
                high, low = parts(whole[even, : 128 * p])
                whole_high[even, : 128 * p] = high
                whole_low[even, : 128 * p] = low
                change = nn(link[0], high) + (nn(link[0], low) + nn(link[1], high))
                high, low = parts(whole[odd, : 128 * p] - change)
                whole_high[odd, : 128 * p] = high
                whole_low[odd, : 128 * p] = low
        return links

    def times(a_high, a_low, b_high, b_low):
        m = a_high.shape[0]
        both = nt(jnp.concatenate([a_high, a_low], axis=0), b_high)
        return both[:m] + (both[m:] + nt(a_high, b_low))

    def start_of(half, links):
        held = []
        for p in range(4 * half, 4 * half + 4):
            right = unpack_pair(reduced[0, p], reduced[1, p])
            first = right[:, :64]
            change = times(*parts(first), *links[p - 4 * half])
            held.append(jnp.concatenate([first, right[:, 64:] - change], axis=1))
        return held

    def solve(half, held):
        highs, lows = [], []
        for i in range(4):
            p = 4 * half + i
            solved[p] = held[i]
            high, low = parts(held[i])
            highs.append(high)
            lows.append(low)
            if i < 3:
                rows = slice(128 * (p + 1), 512 * (half + 1))
                at = slice(128 * p, 128 * (p + 1))
                change = times(high, low, whole_high[rows, at], whole_low[rows, at])
                for m in range(i + 1, 4):
                    first = 128 * (m - i - 1)
                    held[m] = held[m] - change[:, first : first + 128]
        return jnp.concatenate(highs, axis=1), jnp.concatenate(lows, axis=1)

    others(0)
    to_sibling(0)
    from_sibling(0)
    links = prepare(0)
    pair(0).wait_recv()
    high, low = solve(0, start_of(0, links))

    others(1)
    all_col(under_parts, 1).wait_recv()
    for p in range(8):
        at = slice(128 * p, 128 * (p + 1))
        under_high[:, at], under_low[:, at] = parts(
            unpack_pair(under_parts[2 * p], under_parts[2 * p + 1])
        )
    later = times(high, low, under_high[:, :512], under_low[:, :512])
    from_sibling(1)
    links = prepare(1)
    known = times(high, low, whole_high[512:, :512], whole_low[512:, :512])

    all_col(next_parts, 2).wait_recv()
    sum_2 = next_parts[0]
    for k in range(1, 16):
        sum_2 = sum_2 + next_parts[k]
    later = next_target[...] - unpack(sum_2) - later

    for i, buffer in enumerate((panel_parts, under_parts, next_parts)):
        all_col(buffer, i).wait_send()
    z_all(7, 0).wait_send()
    pair(0).wait_send()

    def own_sent(n):
        pltpu.make_async_remote_copy(
            src_ref=whole.at[pl.ds(0, 112), pl.ds(0, 128 * n)],
            dst_ref=whole.at[pl.ds(0, 112), pl.ds(0, 128 * n)],
            send_sem=a_send.at[0],
            recv_sem=a_recv.at[0],
            device_id=sibling,
            device_id_type=MESH,
        ).wait_send()

    by_width(z + core, own_sent)

    @pl.loop(0, 8)
    def _(at):
        def one(n):
            c_copy(n, at, 0, 64).wait_send()
            pl.when(at != z)(lambda: b_all(n, at).wait_send())

        by_width(at + core, one)

    to_sibling(1)
    pair(1).wait_recv()
    held = [
        start - known[:, 128 * i : 128 * (i + 1)] for i, start in enumerate(start_of(1, links))
    ]
    high, low = solve(1, held)
    mine = solved[z]
    own = jnp.where(core == 0, mine[:, :64], mine[:, 64:])
    remainder = later - times(high, low, under_high[:, 512:], under_low[:, 512:])
    out_ref[...] = jnp.concatenate([own, remainder], axis=1)
    pair(1).wait_send()


def local(*args):
    width = args[0].shape[1]
    chunks = width // CHUNK
    dma = pltpu.SemaphoreType.DMA
    out = pl.pallas_call(
        kernel,
        out_shape=pltpu.VMEM((64, 128), F32),
        in_specs=[pl.BlockSpec(memory_space=pltpu.HBM)] * 8,
        out_specs=pl.BlockSpec(memory_space=pltpu.VMEM),
        scratch_shapes=[
            pltpu.VMEM((192, width), F32),
            pltpu.VMEM((64, 1024), F32),
            pltpu.VMEM((4, 64, 64), F32),
            pltpu.VMEM((1024, 1024), F32),
            pltpu.VMEM((1024, 1024), BF16),
            pltpu.VMEM((1024, 1024), BF16),
            pltpu.VMEM((64, 1024), BF16),
            pltpu.VMEM((64, 1024), BF16),
            pltpu.VMEM((8, 64, 128), F32),
            pltpu.VMEM((16, 32, 128), F32),
            pltpu.VMEM((16, 32, 128), F32),
            pltpu.VMEM((16, 32, 128), F32),
            pltpu.VMEM((2, 8, 32, 128), F32),
            dma((chunks,)),
            dma((2,)),
            dma((3,)),
            dma((3,)),
            dma((1,)),
            dma((2,)),
            dma((2,)),
            dma((2,)),
            dma((1,)),
            dma((8,)),
            dma((8,)),
            dma((8,)),
            dma((8,)),
            dma((8,)),
        ],
        compiler_params=pltpu.CompilerParams(
            collective_id=0, has_side_effects=True, vmem_limit_bytes=60 * 1024 * 1024
        ),
    )(*args)
    return out[:, :64], out[:, 64:]


def solution(mesh):
    return jax.shard_map(
        local,
        mesh=mesh,
        in_specs=(
            P("row", "col"),
            P(None, "col"),
            P("row", None),
            P("row", None),
            P(None, "row"),
            P("row", "col"),
            P("row", "col"),
            P(None, "row"),
        ),
        out_specs=(P(None, "row"), P(None, "row")),
        check_vma=False,
    )
```

time: 36.8 us -> 34 us (0.924)
  Pallas kernels: 34.5 us -> 32.6 us
  local copies, waits for them, and re-layouts: 1.53 us -> 0.69 us
    pallas_call x1, Pallas kernels: 34.5 us -> 32.6 us  [local(): pl.pallas_call(kernel, out_shape=pltpu.VMEM((64, 128), F32), in_specs=[pl...]
    slice x1, local copies, waits for them, and re-layouts: 1.53 us -> 0.69 us  [local(): return (out[:, :64], out[:, 64:])]
where the time goes in v3:
time: 34 us; the launch traced here: 33.9 us
  Pallas kernels  32.6 us (96%)
  local copies, waits for them, and re-layouts  0.69 us (2%)
  between operations  0.64 us (2%)
    pallas_call x1, Pallas kernels, local(): pl.pallas_call(kernel, out_shape=pltpu.VMEM((64, 128), F32), in_specs=[pl...  32.6 us
    slice x1, local copies, waits for them, and re-layouts, local(): return (out[:, :64], out[:, 64:])  0.69 us

profile of v3, /device:TPU:1, one launch (start us, length us, event | category | flops | bytes accessed | tf_op | source)
XLA Modules:
  0.0 33.9 jit_solution(13964826712335581453)
XLA Ops:
  0.6 32.6 %shard_map.95 = f32[64,128]{1,0:T(8,128)S(1)} custom-call(f32[64,12288]{1,0:T(8,128)} %factor_hbm.1, f32[64,12288]{1,0:T(8,128)} %prior_hbm.1, f32[64,1024]{1,0:T(8,128)} %lower_hbm.1, f32[64,64]{1,0:T(8,128)} %inverse_hbm.1, f32[64,64]{1,0:T(8,128)} %target_hbm.1, f32[64,12288]{1,0:T(8,128)} %next_hbm.1, f32[64,64]{1,0:T(8,128)} %under_hbm.1, ...), custom_call_target="tpu_custom_call" | custom-call | tf_op jit(solution)/shard_map/pallas_call | solution.py:461
  33.2 0.7 %fusion = (f32[64,64]{1,0:T(8,128)}, f32[64,64]{1,0:T(8,128)}) fusion(f32[64,128]{1,0:T(8,128)S(1)} %shard_map.95), kind=kLoop, calls=%fused_computation | loop fusion | bytes 65536 | tf_op jit(solution)/shard_map/slice | solution.py:499

commit v4 on v3

--- a/solution.py
+++ b/solution.py
@@ -69,7 +69,10 @@
     under_low,
     solved,
     panel_parts,
-    next_parts,
+    next_out,
+    next_in,
+    next_all,
+    scaled,
     under_parts,
     reduced,
     load_sem,
@@ -141,7 +144,7 @@
             jnp.concatenate([s_high, s_low], axis=0), jnp.concatenate([f_high, f_low], axis=0)
         )
 
-    total = lax.fori_loop(0, 2, add, jnp.zeros((128, 256), F32))
+    total = lax.fori_loop(0, chunks, add, jnp.zeros((128, 256), F32))
     pl.semaphore_wait(barrier, 23)
 
     def over_col(buffer, i, k):
@@ -199,21 +202,35 @@
 
         c_copy(n, z, 0, 64).start()
 
+    sums = (total[:64, :128] + total[64:, 128:]) + (total[:64, 128:] + total[64:, :128])
+    panel_parts[c] = pack(sums[:, :64])
+
+    @pl.loop(1, 16)
+    def _(k):
+        over_col(panel_parts, 0, k).start()
+
     by_width(z + core, send_own)
 
     @pl.loop(1, 16)
     def _(k):
         over_col(under_parts, 1, k).start()
 
-    total = lax.fori_loop(2, chunks, add, total)
-    sums = (total[:64, :128] + total[64:, 128:]) + (total[:64, 128:] + total[64:, :128])
-    panel_parts[c] = pack(sums[:, :64])
+    packed = pack(sums[:, 64:])
+    for k in range(16):
+        next_out[k] = packed[2 * k : 2 * k + 2]
+    next_in[c] = next_out[c]
 
     @pl.loop(1, 16)
     def _(k):
-        over_col(panel_parts, 0, k).start()
-
-    next_parts[c] = pack(sums[:, 64:])
+        to = (c + k) % 16
+        pltpu.make_async_remote_copy(
+            src_ref=next_out.at[to],
+            dst_ref=next_in.at[c],
+            send_sem=col_send.at[2],
+            recv_sem=col_recv.at[2],
+            device_id=(r, to),
+            device_id_type=MESH,
+        ).start()
 
     def b_copy(n, at, d, q):
         tile = 2 * at + core
@@ -270,7 +287,7 @@
     for k in range(1, 16):
         sum_1 = sum_1 + panel_parts[k]
     remaining = target[...] - unpack(sum_1)
-    reduced[core, z] = pack(product(remaining, inverse[...], nt))
+    scaled[...] = product(remaining, inverse[...], nt)
 
     def z_copy(k):
         return pltpu.make_async_remote_copy(
@@ -302,15 +319,26 @@
             device_id_type=MESH,
         )
 
-    @pl.loop(1, 8)
-    def _(k):
-        z_copy(k).start()
-
-    pl.when(z < 4)(lambda: forward(1))
+    def send_scaled(value):
+        reduced[core, z] = pack(value)
+
+        @pl.loop(1, 8)
+        def _(k):
+            z_copy(k).start()
+
+    send_scaled(scaled[...])
+
+    all_col(next_in, 2).wait_recv()
+    sum_2 = next_in[0]
+    for k in range(1, 16):
+        sum_2 = sum_2 + next_in[k]
+    next_all[c] = sum_2
 
     @pl.loop(1, 16)
     def _(k):
-        over_col(next_parts, 2, k).start()
+        over_col(next_all, 3, k).start()
+
+    pl.when(z < 4)(lambda: forward(1))
 
     def others(half):
         @pl.loop(4 * half, 4 * half + 4)
@@ -410,13 +438,11 @@
     links = prepare(1)
     known = times(high, low, whole_high[512:, :512], whole_low[512:, :512])
 
-    all_col(next_parts, 2).wait_recv()
-    sum_2 = next_parts[0]
-    for k in range(1, 16):
-        sum_2 = sum_2 + next_parts[k]
+    all_col(next_all, 3).wait_recv()
+    sum_2 = jnp.concatenate([next_all[k] for k in range(16)], axis=0)
     later = next_target[...] - unpack(sum_2) - later
 
-    for i, buffer in enumerate((panel_parts, under_parts, next_parts)):
+    for i, buffer in enumerate((panel_parts, under_parts, next_out, next_all)):
         all_col(buffer, i).wait_send()
     z_all(7, 0).wait_send()
     pair(0).wait_send()
@@ -474,13 +500,16 @@
             pltpu.VMEM((64, 1024), BF16),
             pltpu.VMEM((8, 64, 128), F32),
             pltpu.VMEM((16, 32, 128), F32),
-            pltpu.VMEM((16, 32, 128), F32),
+            pltpu.VMEM((16, 2, 128), F32),
+            pltpu.VMEM((16, 2, 128), F32),
+            pltpu.VMEM((16, 2, 128), F32),
+            pltpu.VMEM((64, 64), F32),
             pltpu.VMEM((16, 32, 128), F32),
             pltpu.VMEM((2, 8, 32, 128), F32),
             dma((chunks,)),
             dma((2,)),
-            dma((3,)),
-            dma((3,)),
+            dma((4,)),
+            dma((4,)),
             dma((1,)),
             dma((2,)),
             dma((2,)),

time: 34 us -> 33 us (0.971); the launches traced: 33.9 us -> 32.5 us
  Pallas kernels: 32.6 us -> 31.2 us
    pallas_call x1, Pallas kernels: 32.6 us -> 31.2 us  [local(): pl.pallas_call(kernel, out_shape=pltpu.VMEM((64, 128), F32), in_specs=[pl...]
where the time goes in v4:
time: 33 us; the launch traced here: 32.5 us
  Pallas kernels  31.2 us (95%)
  local copies, waits for them, and re-layouts  0.69 us (2%)
  between operations  0.64 us (2%)
    pallas_call x1, Pallas kernels, local(): pl.pallas_call(kernel, out_shape=pltpu.VMEM((64, 128), F32), in_specs=[pl...  31.2 us
    slice x1, local copies, waits for them, and re-layouts, local(): return (out[:, :64], out[:, 64:])  0.69 us

profile of v4, /device:TPU:1, one launch (start us, length us, event | category | flops | bytes accessed | tf_op | source)
XLA Modules:
  0.0 32.5 jit_solution(14356371057059766513)
XLA Ops:
  0.6 31.2 %shard_map.95 = f32[64,128]{1,0:T(8,128)S(1)} custom-call(f32[64,12288]{1,0:T(8,128)} %factor_hbm.1, f32[64,12288]{1,0:T(8,128)} %prior_hbm.1, f32[64,1024]{1,0:T(8,128)} %lower_hbm.1, f32[64,64]{1,0:T(8,128)} %inverse_hbm.1, f32[64,64]{1,0:T(8,128)} %target_hbm.1, f32[64,12288]{1,0:T(8,128)} %next_hbm.1, f32[64,64]{1,0:T(8,128)} %under_hbm.1, ...), custom_call_target="tpu_custom_call" | custom-call | tf_op jit(solution)/shard_map/pallas_call | solution.py:487
  31.9 0.7 %fusion = (f32[64,64]{1,0:T(8,128)}, f32[64,64]{1,0:T(8,128)}) fusion(f32[64,128]{1,0:T(8,128)S(1)} %shard_map.95), kind=kLoop, calls=%fused_computation | loop fusion | bytes 65536 | tf_op jit(solution)/shard_map/slice | solution.py:528

commit v5 on v4

--- a/solution.py
+++ b/solution.py
@@ -144,9 +144,6 @@
             jnp.concatenate([s_high, s_low], axis=0), jnp.concatenate([f_high, f_low], axis=0)
         )
 
-    total = lax.fori_loop(0, chunks, add, jnp.zeros((128, 256), F32))
-    pl.semaphore_wait(barrier, 23)
-
     def over_col(buffer, i, k):
         return pltpu.make_async_remote_copy(
             src_ref=buffer.at[c],
@@ -202,6 +199,19 @@
 
         c_copy(n, z, 0, 64).start()
 
+    total = lax.fori_loop(0, 1, add, jnp.zeros((128, 256), F32))
+
+    @pl.when(z >= 4)
+    def _():
+        pl.semaphore_wait(barrier, 23)
+        by_width(z + core, send_own)
+
+    total = lax.fori_loop(1, chunks, add, total)
+
+    @pl.when(z < 4)
+    def _():
+        pl.semaphore_wait(barrier, 23)
+
     sums = (total[:64, :128] + total[64:, 128:]) + (total[:64, 128:] + total[64:, :128])
     panel_parts[c] = pack(sums[:, :64])
 
@@ -209,7 +219,7 @@
     def _(k):
         over_col(panel_parts, 0, k).start()
 
-    by_width(z + core, send_own)
+    pl.when(z < 4)(lambda: by_width(z + core, send_own))
 
     @pl.loop(1, 16)
     def _(k):

time: 33 us -> 32 us (0.970); the launches traced: 32.5 us -> 31.9 us
  Pallas kernels: 31.2 us -> 30.6 us
    pallas_call x1, Pallas kernels: 31.2 us -> 30.6 us  [local(): pl.pallas_call(kernel, out_shape=pltpu.VMEM((64, 128), F32), in_specs=[pl...]
where the time goes in v5:
time: 32 us; the launch traced here: 31.9 us
  Pallas kernels  30.6 us (96%)
  local copies, waits for them, and re-layouts  0.69 us (2%)
  between operations  0.64 us (2%)
    pallas_call x1, Pallas kernels, local(): pl.pallas_call(kernel, out_shape=pltpu.VMEM((64, 128), F32), in_specs=[pl...  30.6 us
    slice x1, local copies, waits for them, and re-layouts, local(): return (out[:, :64], out[:, 64:])  0.69 us

profile of v5, /device:TPU:1, one launch (start us, length us, event | category | flops | bytes accessed | tf_op | source)
XLA Modules:
  0.0 31.9 jit_solution(1872357722955333900)
XLA Ops:
  0.6 30.6 %shard_map.95 = f32[64,128]{1,0:T(8,128)S(1)} custom-call(f32[64,12288]{1,0:T(8,128)} %factor_hbm.1, f32[64,12288]{1,0:T(8,128)} %prior_hbm.1, f32[64,1024]{1,0:T(8,128)} %lower_hbm.1, f32[64,64]{1,0:T(8,128)} %inverse_hbm.1, f32[64,64]{1,0:T(8,128)} %target_hbm.1, f32[64,12288]{1,0:T(8,128)} %next_hbm.1, f32[64,64]{1,0:T(8,128)} %under_hbm.1, ...), custom_call_target="tpu_custom_call" | custom-call | tf_op jit(solution)/shard_map/pallas_call | solution.py:497
  31.2 0.7 %fusion = (f32[64,64]{1,0:T(8,128)}, f32[64,64]{1,0:T(8,128)}) fusion(f32[64,128]{1,0:T(8,128)S(1)} %shard_map.95), kind=kLoop, calls=%fused_computation | loop fusion | bytes 65536 | tf_op jit(solution)/shard_map/slice | solution.py:538

commit v6 on v5

--- a/solution.py
+++ b/solution.py
@@ -221,10 +221,6 @@
 
     pl.when(z < 4)(lambda: by_width(z + core, send_own))
 
-    @pl.loop(1, 16)
-    def _(k):
-        over_col(under_parts, 1, k).start()
-
     packed = pack(sums[:, 64:])
     for k in range(16):
         next_out[k] = packed[2 * k : 2 * k + 2]
@@ -241,6 +237,10 @@
             device_id=(r, to),
             device_id_type=MESH,
         ).start()
+
+    @pl.loop(1, 16)
+    def _(k):
+        over_col(under_parts, 1, k).start()
 
     def b_copy(n, at, d, q):
         tile = 2 * at + core

time: 32 us -> 31.9 us (level)
  no operation moved by 1% of the time
where the time goes in v6:
time: 31.9 us; the launch traced here: 31.8 us
  Pallas kernels  30.4 us (95%)
  local copies, waits for them, and re-layouts  0.69 us (2%)
  between operations  0.64 us (2%)
    pallas_call x1, Pallas kernels, local(): pl.pallas_call(kernel, out_shape=pltpu.VMEM((64, 128), F32), in_specs=[pl...  30.4 us
    slice x1, local copies, waits for them, and re-layouts, local(): return (out[:, :64], out[:, 64:])  0.69 us

profile of v6, /device:TPU:1, one launch (start us, length us, event | category | flops | bytes accessed | tf_op | source)
XLA Modules:
  0.0 31.8 jit_solution(906289732216028394)
XLA Ops:
  0.6 30.4 %shard_map.95 = f32[64,128]{1,0:T(8,128)S(1)} custom-call(f32[64,12288]{1,0:T(8,128)} %factor_hbm.1, f32[64,12288]{1,0:T(8,128)} %prior_hbm.1, f32[64,1024]{1,0:T(8,128)} %lower_hbm.1, f32[64,64]{1,0:T(8,128)} %inverse_hbm.1, f32[64,64]{1,0:T(8,128)} %target_hbm.1, f32[64,12288]{1,0:T(8,128)} %next_hbm.1, f32[64,64]{1,0:T(8,128)} %under_hbm.1, ...), custom_call_target="tpu_custom_call" | custom-call | tf_op jit(solution)/shard_map/pallas_call | solution.py:497
  31.1 0.7 %fusion = (f32[64,64]{1,0:T(8,128)}, f32[64,64]{1,0:T(8,128)}) fusion(f32[64,128]{1,0:T(8,128)S(1)} %shard_map.95), kind=kLoop, calls=%fused_computation | loop fusion | bytes 65536 | tf_op jit(solution)/shard_map/slice | solution.py:538
